TPU v7x, 512 devices: a whole 4x8x8 slice. The times are simulated.
512 devices in a mesh: space: 128 (over x, y, z_lo), vz: 4 (over z_hi, core).
Axes of the slice: x: 4, y: 8, z: 8 (z_hi: 2, z_lo: 4; z = z_hi * 4 + z_lo), core: 2. Of those that a mesh axis runs over, the one named last changes fastest.
Arguments:
- distribution: float32 [48, 256, 8, 2304], P('vz', 'space'), may hold values from 0 to 6, as said below
- collision_rate: float32 [256, 8], P('space'), may hold values from 0.5 to 2
Outputs:
- new_distribution: float32 [48, 256, 8, 2304], P('vz', 'space')
Inputs may be any that keep to these rules, and one draw needn't show every extreme that they name: `distribution`: every entry is positive.
All inputs are finite; a program needn't handle non-finite values.
Results may differ from a plain program's by a relative error of at most 0.000056.
Values sent between devices are 32-bit elements; how exact they have to be, the bound alone decides.
No kernel may reach another device: no remote copies, remote signals or barrier semaphores. Data moves between devices by JAX's collectives and lax.ppermute only.
A program may use at most 64 MiB of HBM per device.

v0:
```python
import jax
import jax.numpy as jnp
from jax import lax
from jax.sharding import PartitionSpec as P

V = 48
SWEEPS = 3
vel_max = 4.5
step_ratio = 0.1
collision_scale = 0.004
relax_scale = 0.5


def with_halo(block, sides, width, periodic):
    for axis, dim in sides:
        count = lax.axis_size(axis)
        forward = [(i, i + 1) for i in range(count - 1)]
        if periodic:
            forward.append((count - 1, 0))
        backward = [(target, source) for source, target in forward]
        low = lax.ppermute(
            lax.slice_in_dim(block, block.shape[dim] - width, None, axis=dim), axis, forward
        )
        high = lax.ppermute(lax.slice_in_dim(block, 0, width, axis=dim), axis, backward)
        block = jnp.concatenate([low, block, high], axis=dim)
    return block


def grid_speeds(position):
    return vel_max * (2.0 * position + 1.0 - V) / V


def velocity_columns():
    grid_values = grid_speeds(jnp.arange(V, dtype=jnp.float32))
    return (jnp.repeat(grid_values, V), jnp.tile(grid_values, V))


def beam_warming(middle, near_cells, far_cells, magnitude):
    return (
        middle
        - 0.5 * magnitude * (3.0 * middle - 4.0 * near_cells + far_cells)
        + 0.5 * magnitude * magnitude * (middle - 2.0 * near_cells + far_cells)
    )


def roll_transport(field_data, speed_cols, axis_id):
    positive = speed_cols > 0
    near_cells = jnp.where(
        positive, jnp.roll(field_data, 1, axis_id), jnp.roll(field_data, -1, axis_id)
    )
    far_cells = jnp.where(
        positive, jnp.roll(field_data, 2, axis_id), jnp.roll(field_data, -2, axis_id)
    )
    return beam_warming(field_data, near_cells, far_cells, step_ratio * jnp.abs(speed_cols))


def combine_planes(partial_value, vertical_speeds):
    zero_moment = partial_value[0]
    return jnp.stack(
        [
            jnp.sum(zero_moment, 0),
            jnp.sum(partial_value[1], 0),
            jnp.sum(partial_value[2], 0),
            jnp.sum(vertical_speeds * zero_moment, 0),
            jnp.sum(partial_value[3] + vertical_speeds * vertical_speeds * zero_moment, 0),
        ]
    )


def cell_state(moment_totals):
    grid_spacing = 2.0 * vel_max / V
    unnormalised_mass = moment_totals[0]
    drift_velocity_x = moment_totals[1] / unnormalised_mass
    drift_velocity_y = moment_totals[2] / unnormalised_mass
    drift_velocity_z = moment_totals[3] / unnormalised_mass
    thermal_energy = (
        moment_totals[4] / unnormalised_mass
        - drift_velocity_x * drift_velocity_x
        - drift_velocity_y * drift_velocity_y
        - drift_velocity_z * drift_velocity_z
    ) / 3.0
    return (
        unnormalised_mass * grid_spacing**3,
        drift_velocity_x,
        drift_velocity_y,
        drift_velocity_z,
        thermal_energy,
    )


def maxwellian(cell_entries, velocity_x_grid, velocity_y_grid, vertical_speeds):
    mass_density, drift_velocity_x, drift_velocity_y, drift_velocity_z, thermal_energy = (
        cell_entries
    )
    squared_spread = (
        (velocity_x_grid - drift_velocity_x) ** 2
        + (velocity_y_grid - drift_velocity_y) ** 2
        + (vertical_speeds - drift_velocity_z) ** 2
    )
    return (
        mass_density
        * (2.0 * jnp.pi * thermal_energy) ** (-1.5)
        * jnp.exp(-squared_spread / (2.0 * thermal_energy))
    )


def velocity_shifts(middle):
    zero_row = jnp.zeros(middle.shape[:-1] + (V,), middle.dtype)
    zero_one = jnp.zeros(middle.shape[:-1] + (1,), middle.dtype)
    upper_x_neighbour = jnp.concatenate([middle[..., V:], zero_row], axis=-1)
    lower_x_neighbour = jnp.concatenate([zero_row, middle[..., :-V]], axis=-1)
    upper_y_neighbour = jnp.concatenate([middle[..., 1:], zero_one], axis=-1)
    lower_y_neighbour = jnp.concatenate([zero_one, middle[..., :-1]], axis=-1)
    return (upper_x_neighbour, lower_x_neighbour, upper_y_neighbour, lower_y_neighbour)


def relaxation_pass(
    bordered_grid,
    forcing_term,
    diagonal_factor,
    vertical_speeds,
    cell_entries,
    collide_rate,
    velocity_x_grid,
    velocity_y_grid,
    upper_mask,
    lower_mask,
):
    mass_density, drift_velocity_x, drift_velocity_y, drift_velocity_z, thermal_energy = (
        cell_entries
    )
    grid_spacing = 2.0 * vel_max / V
    stiffness_factor = thermal_energy / (grid_spacing * grid_spacing)
    half_timestep = 0.5 / grid_spacing
    middle = bordered_grid[1:-1]
    upper_x_neighbour, lower_x_neighbour, upper_y_neighbour, lower_y_neighbour = velocity_shifts(
        middle
    )
    running_total = forcing_term + collide_rate * (
        (stiffness_factor + (velocity_x_grid + grid_spacing - drift_velocity_x) * half_timestep)
        * upper_x_neighbour
        + (stiffness_factor - (velocity_x_grid - grid_spacing - drift_velocity_x) * half_timestep)
        * lower_x_neighbour
    )
    running_total = running_total + collide_rate * (
        (stiffness_factor + (velocity_y_grid + grid_spacing - drift_velocity_y) * half_timestep)
        * upper_mask
        * upper_y_neighbour
        + (stiffness_factor - (velocity_y_grid - grid_spacing - drift_velocity_y) * half_timestep)
        * lower_mask
        * lower_y_neighbour
    )
    running_total = running_total + collide_rate * (
        (stiffness_factor + (vertical_speeds + grid_spacing - drift_velocity_z) * half_timestep)
        * bordered_grid[2:]
        + (stiffness_factor - (vertical_speeds - grid_spacing - drift_velocity_z) * half_timestep)
        * bordered_grid[:-2]
    )
    return running_total / diagonal_factor


def shards(distribution, collision_rate):
    plane_count, column_count, row_count, velocity_width = distribution.shape
    half_width = velocity_width // 2
    velocity_x_grid, velocity_y_grid = velocity_columns()
    magnitude = step_ratio * jnp.abs(velocity_x_grid)
    extended = with_halo(distribution, (("space", 1),), 2, True)
    forward = beam_warming(
        distribution[..., half_width:],
        extended[:, 1 : column_count + 1, :, half_width:],
        extended[:, :column_count, :, half_width:],
        magnitude[half_width:],
    )
    backward = beam_warming(
        distribution[..., :half_width],
        extended[:, 3 : column_count + 3, :, :half_width],
        extended[:, 4 : column_count + 4, :, :half_width],
        magnitude[:half_width],
    )
    swept_x = jnp.concatenate([backward, forward], axis=-1)
    transported = roll_transport(swept_x, velocity_y_grid, 2)
    weights = jnp.stack(
        [
            jnp.ones_like(velocity_x_grid),
            velocity_x_grid,
            velocity_y_grid,
            velocity_x_grid * velocity_x_grid + velocity_y_grid * velocity_y_grid,
        ],
        axis=1,
    )
    partial_value = jnp.einsum(
        "zxyk,kw->wzxy", distribution, weights, precision=lax.Precision.HIGHEST
    )
    first_plane = lax.axis_index("vz") * plane_count
    local_speeds = grid_speeds(
        (first_plane + jnp.arange(plane_count, dtype=jnp.int32)).astype(jnp.float32)
    )
    moment_totals = lax.psum(combine_planes(partial_value, local_speeds[:, None, None]), "vz")
    cell_entries = tuple(
        (entry_array[None, :, :, None] for entry_array in cell_state(moment_totals))
    )
    grid_spacing = 2.0 * vel_max / V
    pointwise_rate = collision_rate[None, :, :, None]
    collide_rate = collision_scale * pointwise_rate
    relaxation_rate = relax_scale * pointwise_rate
    stiffness_factor = cell_entries[4] / (grid_spacing * grid_spacing)
    diagonal_factor = 1.0 + relaxation_rate + 6.0 * collide_rate * stiffness_factor
    index_y = jnp.arange(velocity_width, dtype=jnp.int32) % V
    upper_mask = (index_y < V - 1).astype(jnp.float32)
    lower_mask = (index_y > 0).astype(jnp.float32)
    vertical_speeds = local_speeds[:, None, None, None]
    forcing_term = transported + relaxation_rate * maxwellian(
        cell_entries, velocity_x_grid, velocity_y_grid, vertical_speeds
    )
    current_guess = transported
    for sweep_id in range(SWEEPS):
        bordered_grid = with_halo(current_guess, (("vz", 0),), 1, False)
        current_guess = relaxation_pass(
            bordered_grid,
            forcing_term,
            diagonal_factor,
            vertical_speeds,
            cell_entries,
            collide_rate,
            velocity_x_grid,
            velocity_y_grid,
            upper_mask,
            lower_mask,
        )
    return current_guess


def solution(mesh):
    return jax.shard_map(
        shards,
        mesh=mesh,
        in_specs=(P("vz", "space", None, None), P("space", None)),
        out_specs=P("vz", "space", None, None),
        check_vma=False,
    )
```

profile of v0, /device:TPU:1, one launch (start us, length us, event | category | flops | bytes accessed | tf_op | source)
XLA Modules:
  0.0 159.6 jit_solution(4560179693643808710)
XLA Ops:
  0.0 13.5 %collective-permute-start = (f32[12,2,8,2304]{3,2,1,0:T(8,128)}, f32[12,2,8,2304]{3,2,1,0:T(8,128)S(1)}, u32[]{:S(2)}, u32[]{:S(2)}) collective-permute-start(f32[12,2,8,2304]{3,2,1,0:T(8,128)} %param.2), channel_id=1, source_target_pairs={{4,0},{8,4},{12,8},{16,12},{20,16},{24,20},{28,24},{32,28},{36,32}... | collective-permute-start | bytes 5308424 | tf_op jit(solution)/shard_map/ppermute | solution.py:24
  13.5 1.9 %collective-permute-start.1 = (f32[12,2,8,2304]{3,2,1,0:T(8,128)}, f32[12,2,8,2304]{3,2,1,0:T(8,128)}, u32[]{:S(2)}, u32[]{:S(2)}) collective-permute-start(f32[12,2,8,2304]{3,2,1,0:T(8,128)} %param.2), channel_id=1, source_target_pairs={{0,4},{4,8},{8,12},{12,16},{16,20},{20,24},{24,28},{28,32},{32,36}... | collective-permute-start | bytes 5308424 | tf_op jit(solution)/shard_map/ppermute | solution.py:21
  15.5 0.6 broadcast_add_fusion.4
  16.1 0.6 add_multiply_fusion.1
  16.7 0.1 stack_tile.5
  16.8 0.1 broadcast_in_dim.25
  16.8 0.7 stack_reshape.5
  17.5 0.0 copy-done.1
  17.5 0.0 copy-done.2
  17.5 0.7 multiply_add_fusion.6
  18.3 0.0 copy-start
  18.3 10.0 %fusion = f32[4,12,2,8]{1,0,3,2:T(4,128)S(1)} fusion(f32[12,2,8,2304]{3,2,1,0:T(8,128)} %param.2, f32[2304,1]{0,1:T(1,128)S(1)} %multiply_add_fusion.6, f32[2304,1]{0,1:T(1,128)S(1)} %stack_tile.5, f32[2304,1]{0,1:T(1,128)} %stack_reshape.5, f32[4]{0:T(128)S(1)} %pad.24.clone), kind=kOutput, calls=%fused_computation.17 | convolution fusion | flops 21261312 | bytes 1800208 | tf_op jit(solution)/shard_map/zxyk,kw->wzxy/dot_general | solution.py:191
  28.2 0.8 slice_reduce_fusion
  29.0 0.7 reduce_sum.45
  29.7 1.2 constant_dynamic-update-slice_fusion.4
  30.9 1.3 constant_dynamic-update-slice_fusion.3
  32.2 1.3 constant_dynamic-update-slice_fusion.2
  33.4 0.8 add_reduce_fusion
  34.2 0.5 constant_dynamic-update-slice_fusion.1
  34.7 0.6 constant_dynamic-update-slice_fusion
  35.3 58.7 %psum.7 = f32[5,2,8]{2,1,0:T(2,128)S(1)} all-reduce(f32[5,2,8]{2,1,0:T(2,128)} %constant_dynamic-update-slice_fusion), channel_id=1, replica_groups=mesh['space'=128,'vz'=4] {'vz'}, use_global_device_ids=true, to_apply=%region_5.6 | all-reduce | flops 80 | bytes 640 | tf_op jit(solution)/shard_map/psum | solution.py:198
  94.0 0.6 bitcast_multiply_fusion
  94.6 1.3 broadcast_multiply_fusion.3
  95.9 0.6 copy-done.10
  96.5 1.4 multiply_add_fusion.7
  97.8 0.8 tile.38
  98.6 1.4 reshape.331
  100.1 1.4 copy.6
  101.4 1.4 copy.7
  102.8 1.4 copy.5
  104.2 0.7 broadcast_add_fusion.3
  105.0 0.9 multiply_add_fusion.4
  105.8 0.0 collective-permute-done
  105.9 0.0 collective-permute-done.1
  105.9 0.0 copy-done
  105.9 1.9 %multiply_add_fusion.2 = (f32[12,2,8,1152]{3,2,1,0:T(8,128)S(1)}, f32[12,2,8,1152]{3,2,1,0:T(8,128)S(1)}) fusion(f32[12,2,8,2304]{3,2,1,0:T(8,128)} %collective-permute-done.1, f32[12,2,8,2304]{3,2,1,0:T(8,128)S(1)} %copy-done, f32[1152]{0:T(1024)S(1)} %get-tuple-element.53, f32[1152]{0:T(1024)S(1)} %get-tuple-element.51, f32[1152]{0:T(1024)S(1)} %get-tuple-element.52, ...), kind=kLoop, calls=%fused_computation.53 | loop fusion | flops 5308416 | bytes 10649600 | tf_op jit(solution)/shard_map/add | solution.py:40
  107.8 0.3 fusion.26
  108.1 0.3 fusion.24
  108.4 0.4 fusion.4
  108.7 0.4 fusion.2
  109.1 2.0 %multiply_add_fusion.1 = f32[12,2,8,2304]{3,2,1,0:T(8,128)S(1)} fusion(f32[12,2,2,2304]{3,2,1,0:T(2,128)S(1)} %get-tuple-element.37, f32[12,2,6,2304]{3,2,1,0:T(8,128)S(1)} %get-tuple-element.39, f32[12,2,6,2304]{3,2,1,0:T(8,128)S(1)} %get-tuple-element.38, f32[12,2,2,2304]{3,2,1,0:T(2,128)S(1)} %get-tuple-element.36, ...), kind=kLoop, calls=%fused_computation.50 | loop fusion | flops 7962624 | bytes 10637568 | tf_op jit(solution)/shard_map/add | solution.py:40
  111.2 0.6 fusion.59
  111.8 2.1 %collective-permute-start.2 = (f32[1,2,8,2304]{3,2,1,0:T(8,128)S(1)}, f32[1,2,8,2304]{3,2,1,0:T(8,128)S(1)}, u32[]{:S(2)}, u32[]{:S(2)}) collective-permute-start(f32[1,2,8,2304]{3,2,1,0:T(8,128)S(1)} %get-tuple-element.30), channel_id=1, source_target_pairs={{1,0},{2,1},{3,2},{5,4},{6,5},{7,6},{9,8},{10,9},{11,10},{13,12},{... | collective-permute-start | bytes 442376 | tf_op jit(solution)/shard_map/ppermute | solution.py:24
  113.8 0.0 copy-start.4
  113.9 7.7 %collective-permute-start.3 = (f32[1,2,8,2304]{3,2,1,0:T(8,128)S(1)}, f32[1,2,8,2304]{3,2,1,0:T(8,128)S(1)}, u32[]{:S(2)}, u32[]{:S(2)}) collective-permute-start(f32[1,2,8,2304]{3,2,1,0:T(8,128)S(1)} %get-tuple-element.31), channel_id=1, source_target_pairs={{0,1},{1,2},{2,3},{4,5},{5,6},{6,7},{8,9},{9,10},{10,11},{12,13},{... | collective-permute-start | bytes 442376 | tf_op jit(solution)/shard_map/ppermute | solution.py:21
  121.6 0.6 fusion.58
  122.2 0.3 collective-permute-done.2
  122.5 1.4 collective-permute-done.3
  123.9 0.0 copy-done.5
  124.0 2.1 %fusion.22 = f32[12,2,8,2304]{3,2,1,0:T(8,128)S(1)} fusion(f32[12,2,8,2304]{3,2,1,0:T(8,128)S(1)} %multiply_add_fusion.1, f32[1,2,8,2304]{3,2,1,0:T(8,128)S(1)} %collective-permute-done.3, f32[1,2,8,2304]{3,2,1,0:T(8,128)S(1)} %collective-permute-done.2, f32[12,2,8,2303]{3,2,1,0:T(8,128)S(1)} %get-tuple-element.29, ...), kind=kLoop, calls=%fused_computation.44 | loop fusion | flops 10616832 | bytes 11576384 | tf_op jit(solution)/shard_map/div | solution.py:159
  126.1 0.6 fusion.56
  126.7 1.9 %collective-permute-start.4 = (f32[1,2,8,2304]{3,2,1,0:T(8,128)S(1)}, f32[1,2,8,2304]{3,2,1,0:T(8,128)S(1)}, u32[]{:S(2)}, u32[]{:S(2)}) collective-permute-start(f32[1,2,8,2304]{3,2,1,0:T(8,128)S(1)} %get-tuple-element.24), channel_id=1, source_target_pairs={{1,0},{2,1},{3,2},{5,4},{6,5},{7,6},{9,8},{10,9},{11,10},{13,12},{... | collective-permute-start | bytes 442376 | tf_op jit(solution)/shard_map/ppermute | solution.py:24
  128.6 8.6 %collective-permute-start.5 = (f32[1,2,8,2304]{3,2,1,0:T(8,128)S(1)}, f32[1,2,8,2304]{3,2,1,0:T(8,128)S(1)}, u32[]{:S(2)}, u32[]{:S(2)}) collective-permute-start(f32[1,2,8,2304]{3,2,1,0:T(8,128)S(1)} %get-tuple-element.25), channel_id=1, source_target_pairs={{0,1},{1,2},{2,3},{4,5},{5,6},{6,7},{8,9},{9,10},{10,11},{12,13},{... | collective-permute-start | bytes 442376 | tf_op jit(solution)/shard_map/ppermute | solution.py:21
  137.2 0.6 fusion.55
  137.8 0.2 collective-permute-done.4
  138.0 2.3 %collective-permute-done.5 = f32[1,2,8,2304]{3,2,1,0:T(8,128)S(1)} collective-permute-done((f32[1,2,8,2304]{3,2,1,0:T(8,128)S(1)}, f32[1,2,8,2304]{3,2,1,0:T(8,128)S(1)}, u32[]{:S(2)}, u32[]{:S(2)}) %collective-permute-start.5) | collective-permute-done | bytes 147488 | tf_op jit(solution)/shard_map/ppermute | solution.py:21
  140.3 2.0 %fusion.16 = f32[12,2,8,2304]{3,2,1,0:T(8,128)S(1)} fusion(f32[12,2,8,2304]{3,2,1,0:T(8,128)S(1)} %fusion.22, f32[1,2,8,2304]{3,2,1,0:T(8,128)S(1)} %collective-permute-done.5, f32[1,2,8,2304]{3,2,1,0:T(8,128)S(1)} %collective-permute-done.4, f32[12,2,8,2303]{3,2,1,0:T(8,128)S(1)} %get-tuple-element.23, f32[12,2,8,2303]{3,2,1,0:T(8,128)S(1)} %get-tuple-element.22, ...), kind=kLoop, calls=%fused_computation.36 | loop fusion | flops 10616832 | bytes 13345856 | tf_op jit(solution)/shard_map/div | solution.py:159
  142.4 0.6 fusion.53
  143.0 1.9 %collective-permute-start.6 = (f32[1,2,8,2304]{3,2,1,0:T(8,128)S(1)}, f32[1,2,8,2304]{3,2,1,0:T(8,128)S(1)}, u32[]{:S(2)}, u32[]{:S(2)}) collective-permute-start(f32[1,2,8,2304]{3,2,1,0:T(8,128)S(1)} %get-tuple-element.18), channel_id=1, source_target_pairs={{1,0},{2,1},{3,2},{5,4},{6,5},{7,6},{9,8},{10,9},{11,10},{13,12},{... | collective-permute-start | bytes 442376 | tf_op jit(solution)/shard_map/ppermute | solution.py:24
  145.0 8.4 %collective-permute-start.7 = (f32[1,2,8,2304]{3,2,1,0:T(8,128)S(1)}, f32[1,2,8,2304]{3,2,1,0:T(8,128)S(1)}, u32[]{:S(2)}, u32[]{:S(2)}) collective-permute-start(f32[1,2,8,2304]{3,2,1,0:T(8,128)S(1)} %get-tuple-element.19), channel_id=1, source_target_pairs={{0,1},{1,2},{2,3},{4,5},{5,6},{6,7},{8,9},{9,10},{10,11},{12,13},{... | collective-permute-start | bytes 442376 | tf_op jit(solution)/shard_map/ppermute | solution.py:21
  153.4 0.6 fusion.52
  154.0 0.4 collective-permute-done.6
  154.3 2.3 %collective-permute-done.7 = f32[1,2,8,2304]{3,2,1,0:T(8,128)S(1)} collective-permute-done((f32[1,2,8,2304]{3,2,1,0:T(8,128)S(1)}, f32[1,2,8,2304]{3,2,1,0:T(8,128)S(1)}, u32[]{:S(2)}, u32[]{:S(2)}) %collective-permute-start.7) | collective-permute-done | bytes 147488 | tf_op jit(solution)/shard_map/ppermute | solution.py:21
  156.7 2.9 %fusion.10 = f32[12,2,8,2304]{3,2,1,0:T(8,128)} fusion(f32[12,2,8,2304]{3,2,1,0:T(8,128)S(1)} %fusion.16, f32[1,2,8,2304]{3,2,1,0:T(8,128)S(1)} %collective-permute-done.7, f32[1,2,8,2304]{3,2,1,0:T(8,128)S(1)} %collective-permute-done.6, f32[12,2,8,2303]{3,2,1,0:T(8,128)S(1)} %get-tuple-element.17, f32[12,2,8,2303]{3,2,1,0:T(8,128)S(1)} %get-tuple-element.16, ...), kind=kLoop, calls=%fused_computation.28 | loop fusion | flops 10616832 | bytes 13345856 | tf_op jit(solution)/shard_map/div | solution.py:159
  (25 shorter events, 0.1 us)
Async XLA Ops:
  0.0 105.8 %collective-permute-start = (f32[12,2,8,2304]{3,2,1,0:T(8,128)}, f32[12,2,8,2304]{3,2,1,0:T(8,128)S(1)}, u32[]{:S(2)}, u32[]{:S(2)}) collective-permute-start(f32[12,2,8,2304]{3,2,1,0:T(8,128)} %param.2), channel_id=1, source_target_pairs={{4,0},{8,4},{12,8},{16,12},{20,16},{24,20},{28,24},{32,28},{36,32}... | collective-permute-start | bytes 5308424 | tf_op jit(solution)/shard_map/ppermute | solution.py:24
  13.5 92.3 %collective-permute-start.1 = (f32[12,2,8,2304]{3,2,1,0:T(8,128)}, f32[12,2,8,2304]{3,2,1,0:T(8,128)}, u32[]{:S(2)}, u32[]{:S(2)}) collective-permute-start(f32[12,2,8,2304]{3,2,1,0:T(8,128)} %param.2), channel_id=1, source_target_pairs={{0,4},{4,8},{8,12},{12,16},{16,20},{20,24},{24,28},{28,32},{32,36}... | collective-permute-start | bytes 5308424 | tf_op jit(solution)/shard_map/ppermute | solution.py:21
  16.7 0.9 copy-start.1
  16.8 0.7 copy-start.2
  18.3 87.6 %copy-start = (f32[12,2,8,2304]{3,2,1,0:T(8,128)S(1)}, f32[12,2,8,2304]{3,2,1,0:T(8,128)}, u32[]{:S(2)}) copy-start(f32[12,2,8,2304]{3,2,1,0:T(8,128)} %param.2) | copy-start | bytes 5308420
  95.9 0.6 copy-start.10
  111.8 10.8 %collective-permute-start.2 = (f32[1,2,8,2304]{3,2,1,0:T(8,128)S(1)}, f32[1,2,8,2304]{3,2,1,0:T(8,128)S(1)}, u32[]{:S(2)}, u32[]{:S(2)}) collective-permute-start(f32[1,2,8,2304]{3,2,1,0:T(8,128)S(1)} %get-tuple-element.30), channel_id=1, source_target_pairs={{1,0},{2,1},{3,2},{5,4},{6,5},{7,6},{9,8},{10,9},{11,10},{13,12},{... | collective-permute-start | bytes 442376 | tf_op jit(solution)/shard_map/ppermute | solution.py:24
  113.8 10.1 %copy-start.3 = (f32[12,2,8]{2,1,0:T(2,128)S(1)}, f32[12,2,8]{2,1,0:T(2,128)}, u32[]{:S(2)}) copy-start(f32[12,2,8]{2,1,0:T(2,128)} %copy.6) | copy-start | bytes 2308
  113.8 10.1 %copy-start.4 = (f32[12,2,8]{2,1,0:T(2,128)S(1)}, f32[12,2,8]{2,1,0:T(2,128)}, u32[]{:S(2)}) copy-start(f32[12,2,8]{2,1,0:T(2,128)} %copy.7) | copy-start | bytes 2308
  113.9 10.1 %copy-start.5 = (f32[12,2,8]{2,1,0:T(2,128)S(1)}, f32[12,2,8]{2,1,0:T(2,128)}, u32[]{:S(2)}) copy-start(f32[12,2,8]{2,1,0:T(2,128)} %copy.5) | copy-start | bytes 2308
  113.9 10.1 %copy-start.6 = (f32[2,8]{1,0:T(2,128)S(1)}, f32[2,8]{1,0:T(2,128)}, u32[]{:S(2)}) copy-start(f32[2,8]{1,0:T(2,128)} %get-tuple-element.61) | copy-start | bytes 196
  113.9 10.1 %copy-start.7 = (f32[2,8]{1,0:T(2,128)S(1)}, f32[2,8]{1,0:T(2,128)}, u32[]{:S(2)}) copy-start(f32[2,8]{1,0:T(2,128)} %get-tuple-element.62) | copy-start | bytes 196
  113.9 10.1 %copy-start.8 = (f32[2,8]{1,0:T(2,128)S(1)}, f32[2,8]{1,0:T(2,128)}, u32[]{:S(2)}) copy-start(f32[2,8]{1,0:T(2,128)} %get-tuple-element.63) | copy-start | bytes 196
  113.9 10.1 %copy-start.9 = (f32[2,8]{1,0:T(2,128)S(1)}, f32[2,8]{1,0:T(2,128)}, u32[]{:S(2)}) copy-start(f32[2,8]{1,0:T(2,128)} %get-tuple-element.65) | copy-start | bytes 196
  113.9 10.0 %collective-permute-start.3 = (f32[1,2,8,2304]{3,2,1,0:T(8,128)S(1)}, f32[1,2,8,2304]{3,2,1,0:T(8,128)S(1)}, u32[]{:S(2)}, u32[]{:S(2)}) collective-permute-start(f32[1,2,8,2304]{3,2,1,0:T(8,128)S(1)} %get-tuple-element.31), channel_id=1, source_target_pairs={{0,1},{1,2},{2,3},{4,5},{5,6},{6,7},{8,9},{9,10},{10,11},{12,13},{... | collective-permute-start | bytes 442376 | tf_op jit(solution)/shard_map/ppermute | solution.py:21
  126.7 11.3 %collective-permute-start.4 = (f32[1,2,8,2304]{3,2,1,0:T(8,128)S(1)}, f32[1,2,8,2304]{3,2,1,0:T(8,128)S(1)}, u32[]{:S(2)}, u32[]{:S(2)}) collective-permute-start(f32[1,2,8,2304]{3,2,1,0:T(8,128)S(1)} %get-tuple-element.24), channel_id=1, source_target_pairs={{1,0},{2,1},{3,2},{5,4},{6,5},{7,6},{9,8},{10,9},{11,10},{13,12},{... | collective-permute-start | bytes 442376 | tf_op jit(solution)/shard_map/ppermute | solution.py:24
  128.6 11.7 %collective-permute-start.5 = (f32[1,2,8,2304]{3,2,1,0:T(8,128)S(1)}, f32[1,2,8,2304]{3,2,1,0:T(8,128)S(1)}, u32[]{:S(2)}, u32[]{:S(2)}) collective-permute-start(f32[1,2,8,2304]{3,2,1,0:T(8,128)S(1)} %get-tuple-element.25), channel_id=1, source_target_pairs={{0,1},{1,2},{2,3},{4,5},{5,6},{6,7},{8,9},{9,10},{10,11},{12,13},{... | collective-permute-start | bytes 442376 | tf_op jit(solution)/shard_map/ppermute | solution.py:21
  143.0 11.3 %collective-permute-start.6 = (f32[1,2,8,2304]{3,2,1,0:T(8,128)S(1)}, f32[1,2,8,2304]{3,2,1,0:T(8,128)S(1)}, u32[]{:S(2)}, u32[]{:S(2)}) collective-permute-start(f32[1,2,8,2304]{3,2,1,0:T(8,128)S(1)} %get-tuple-element.18), channel_id=1, source_target_pairs={{1,0},{2,1},{3,2},{5,4},{6,5},{7,6},{9,8},{10,9},{11,10},{13,12},{... | collective-permute-start | bytes 442376 | tf_op jit(solution)/shard_map/ppermute | solution.py:24
  145.0 11.7 %collective-permute-start.7 = (f32[1,2,8,2304]{3,2,1,0:T(8,128)S(1)}, f32[1,2,8,2304]{3,2,1,0:T(8,128)S(1)}, u32[]{:S(2)}, u32[]{:S(2)}) collective-permute-start(f32[1,2,8,2304]{3,2,1,0:T(8,128)S(1)} %get-tuple-element.19), channel_id=1, source_target_pairs={{0,1},{1,2},{2,3},{4,5},{5,6},{6,7},{8,9},{9,10},{10,11},{12,13},{... | collective-permute-start | bytes 442376 | tf_op jit(solution)/shard_map/ppermute | solution.py:21
where the time goes:
time: 160 us
  blocking collectives  58.7 us (37%)
  starting transfers between devices  46 us (29%)
  other arithmetic  21.2 us (13%)
  local copies, waits for them, and re-layouts  16.4 us (10%)
  matrix products  9.96 us (6%)
  waiting for transfers between devices  6.96 us (4%)
    psum x1, blocking collectives, shards(): lax.psum(combine_planes(partial_value, local_speeds[:, None, None]), 'vz')  58.7 us
    ppermute x4, starting transfers between devices, with_halo(): lax.ppermute(lax.slice_in_dim(block, block.shape[dim] - width, None, axis...  26.6 us
    ppermute x4, starting transfers between devices, with_halo(): lax.ppermute(lax.slice_in_dim(block, 0, width, axis=dim), axis, backward)  19.4 us
    dot_general x1, matrix products, shards(): jnp.einsum('zxyk,kw->wzxy', distribution, weights, precision=lax.Precisio...  9.96 us
    div x3, other arithmetic, relaxation_pass(): return running_total / diagonal_factor  7.02 us
    ppermute x4, waiting for transfers between devices, with_halo(): lax.ppermute(lax.slice_in_dim(block, block.shape[dim] - width, None, axis...  6.09 us
    unnamed x26, local copies, waits for them, and re-layouts  4.9 us
    add x2, other arithmetic, beam_warming(): middle - 0.5 * magnitude * (3.0 * middle - 4.0 * near_cells + far_cells)  3.96 us
  transfers between devices with their start and end apart: 8, of which 6 were waited for; matrix products, arithmetic and copies ran while one was open for 21% of the time, Pallas kernels for 0%

commit v1 on v0

--- a/solution.py
+++ b/solution.py
@@ -195,7 +195,8 @@
     local_speeds = grid_speeds(
         (first_plane + jnp.arange(plane_count, dtype=jnp.int32)).astype(jnp.float32)
     )
-    moment_totals = lax.psum(combine_planes(partial_value, local_speeds[:, None, None]), "vz")
+    message = combine_planes(partial_value, local_speeds[:, None, None])
+    moment_totals = jnp.sum(lax.all_gather(message, "vz"), 0)
     cell_entries = tuple(
         (entry_array[None, :, :, None] for entry_array in cell_state(moment_totals))
     )

time: 160 us -> 162 us (1.012)
  blocking collectives: 58.7 us -> 62.7 us
  local copies, waits for them, and re-layouts: 16.4 us -> 13.5 us
    all_gather x0 -> x1, blocking collectives: none -> 62.7 us  [shards(): moment_totals = jnp.sum(lax.all_gather(message, 'vz'), 0)]
    psum x1 -> x0, blocking collectives: 58.7 us -> none  [shards(): lax.psum(combine_planes(partial_value, local_speeds[:, None, None]), 'vz')]
    unnamed x26 -> x28, local copies, waits for them, and re-layouts: 4.9 us -> 3.24 us
  transfers between devices with their start and end apart: 8 -> 8, of which waited for: 6 -> 6; matrix products, arithmetic and copies ran while one was open for 21% -> 18% of each run, Pallas kernels for 0% -> 0%
where the time goes in v1:
time: 162 us; the launch traced here: 161 us
  blocking collectives  62.7 us (39%)
  starting transfers between devices  45.8 us (28%)
  other arithmetic  21.2 us (13%)
  local copies, waits for them, and re-layouts  13.5 us (8%)
  matrix products  9.96 us (6%)
  waiting for transfers between devices  7.23 us (4%)
    all_gather x1, blocking collectives, shards(): moment_totals = jnp.sum(lax.all_gather(message, 'vz'), 0)  62.7 us
    ppermute x4, starting transfers between devices, with_halo(): lax.ppermute(lax.slice_in_dim(block, block.shape[dim] - width, None, axis...  26.3 us
    ppermute x4, starting transfers between devices, with_halo(): lax.ppermute(lax.slice_in_dim(block, 0, width, axis=dim), axis, backward)  19.5 us
    dot_general x1, matrix products, shards(): jnp.einsum('zxyk,kw->wzxy', distribution, weights, precision=lax.Precisio...  9.96 us
    div x3, other arithmetic, relaxation_pass(): return running_total / diagonal_factor  7.06 us
    ppermute x4, waiting for transfers between devices, with_halo(): lax.ppermute(lax.slice_in_dim(block, block.shape[dim] - width, None, axis...  6.36 us
    add x2, other arithmetic, beam_warming(): middle - 0.5 * magnitude * (3.0 * middle - 4.0 * near_cells + far_cells)  3.95 us
    unnamed x28, local copies, waits for them, and re-layouts  3.24 us
  transfers between devices with their start and end apart: 8, of which 6 were waited for; matrix products, arithmetic and copies ran while one was open for 18% of the time, Pallas kernels for 0%

profile of v1, /device:TPU:1, one launch (start us, length us, event | category | flops | bytes accessed | tf_op | source)
XLA Modules:
  0.0 160.8 jit_solution(8904349352850619390)
XLA Ops:
  0.0 13.5 %collective-permute-start = (f32[12,2,8,2304]{3,2,1,0:T(8,128)}, f32[12,2,8,2304]{3,2,1,0:T(8,128)S(1)}, u32[]{:S(2)}, u32[]{:S(2)}) collective-permute-start(f32[12,2,8,2304]{3,2,1,0:T(8,128)} %param.2), channel_id=1, source_target_pairs={{4,0},{8,4},{12,8},{16,12},{20,16},{24,20},{28,24},{32,28},{36,32}... | collective-permute-start | bytes 5308424 | tf_op jit(solution)/shard_map/ppermute | solution.py:24
  13.5 1.9 %collective-permute-start.1 = (f32[12,2,8,2304]{3,2,1,0:T(8,128)}, f32[12,2,8,2304]{3,2,1,0:T(8,128)}, u32[]{:S(2)}, u32[]{:S(2)}) collective-permute-start(f32[12,2,8,2304]{3,2,1,0:T(8,128)} %param.2), channel_id=1, source_target_pairs={{0,4},{4,8},{8,12},{12,16},{16,20},{20,24},{24,28},{28,32},{32,36}... | collective-permute-start | bytes 5308424 | tf_op jit(solution)/shard_map/ppermute | solution.py:21
  15.5 0.5 broadcast_add_fusion.5
  16.0 0.6 add_multiply_fusion.1
  16.6 0.1 stack_tile.5
  16.7 0.1 broadcast_in_dim.25
  16.8 0.1 stack_reshape.5
  16.9 0.0 copy-start.6
  16.9 0.3 copy-done.1
  17.2 0.2 copy-done.2
  17.4 0.1 copy-done.6
  17.5 0.0 copy-start
  17.5 10.0 %fusion = f32[4,12,2,8]{1,0,3,2:T(4,128)S(1)} fusion(f32[12,2,8,2304]{3,2,1,0:T(8,128)} %param.2, f32[2304,1]{0,1:T(1,128)S(1)} %multiply_add_fusion.6, f32[2304,1]{0,1:T(1,128)S(1)} %stack_tile.5, f32[2304,1]{0,1:T(1,128)} %copy-done.6, f32[4]{0:T(128)S(1)} %pad.24.clone), kind=kOutput, calls=%fused_computation.17 | convolution fusion | flops 21261312 | bytes 1800208 | tf_op jit(solution)/shard_map/zxyk,kw->wzxy/dot_general | solution.py:191
  27.5 0.8 slice_reduce_fusion
  28.2 0.7 reduce_sum.54
  28.9 0.7 constant_dynamic-update-slice_fusion.4
  29.6 0.7 constant_dynamic-update-slice_fusion.3
  30.3 0.7 constant_dynamic-update-slice_fusion.2
  31.0 0.8 add_reduce_fusion
  31.7 62.7 %all-gather = f32[20,2,8]{2,1,0:T(2,128)} all-gather(f32[5,2,8]{2,1,0:T(2,128)S(1)} %constant_dynamic-update-slice_fusion), channel_id=2, replica_groups=mesh['space'=128,'vz'=4] {'vz'}, dimensions={0}, use_global_device_ids=true | all-gather | bytes 1600 | tf_op jit(solution)/shard_map/all_gather | solution.py:199
  94.4 0.7 reduce_sum.59
  95.2 0.6 bitcast_multiply_fusion
  95.8 1.3 broadcast_multiply_fusion.3
  97.1 0.6 copy-done.11
  97.6 1.4 multiply_add_fusion.7
  99.0 0.8 tile.38
  99.8 1.4 reshape.331
  101.2 1.4 copy.11
  102.6 1.4 copy.12
  104.0 1.4 copy.10
  105.4 0.7 broadcast_add_fusion.3
  106.1 0.9 multiply_add_fusion.4
  107.0 0.0 collective-permute-done
  107.0 0.0 collective-permute-done.1
  107.0 0.0 copy-done
  107.0 1.9 %multiply_add_fusion.2 = (f32[12,2,8,1152]{3,2,1,0:T(8,128)S(1)}, f32[12,2,8,1152]{3,2,1,0:T(8,128)S(1)}) fusion(f32[12,2,8,2304]{3,2,1,0:T(8,128)} %collective-permute-done.1, f32[12,2,8,2304]{3,2,1,0:T(8,128)S(1)} %copy-done, f32[1152]{0:T(1024)S(1)} %get-tuple-element.53, f32[1152]{0:T(1024)S(1)} %get-tuple-element.51, f32[1152]{0:T(1024)S(1)} %get-tuple-element.52, ...), kind=kLoop, calls=%fused_computation.53 | loop fusion | flops 5308416 | bytes 10649600 | tf_op jit(solution)/shard_map/add | solution.py:40
  109.0 0.3 fusion.26
  109.3 0.3 fusion.24
  109.5 0.4 fusion.4
  109.9 0.4 fusion.2
  110.3 2.0 %multiply_add_fusion.1 = f32[12,2,8,2304]{3,2,1,0:T(8,128)S(1)} fusion(f32[12,2,2,2304]{3,2,1,0:T(2,128)S(1)} %get-tuple-element.37, f32[12,2,6,2304]{3,2,1,0:T(8,128)S(1)} %get-tuple-element.39, f32[12,2,6,2304]{3,2,1,0:T(8,128)S(1)} %get-tuple-element.38, f32[12,2,2,2304]{3,2,1,0:T(2,128)S(1)} %get-tuple-element.36, ...), kind=kLoop, calls=%fused_computation.50 | loop fusion | flops 7962624 | bytes 10637568 | tf_op jit(solution)/shard_map/add | solution.py:40
  112.3 0.6 fusion.59
  112.9 2.1 %collective-permute-start.2 = (f32[1,2,8,2304]{3,2,1,0:T(8,128)S(1)}, f32[1,2,8,2304]{3,2,1,0:T(8,128)S(1)}, u32[]{:S(2)}, u32[]{:S(2)}) collective-permute-start(f32[1,2,8,2304]{3,2,1,0:T(8,128)S(1)} %get-tuple-element.30), channel_id=1, source_target_pairs={{1,0},{2,1},{3,2},{5,4},{6,5},{7,6},{9,8},{10,9},{11,10},{13,12},{... | collective-permute-start | bytes 442376 | tf_op jit(solution)/shard_map/ppermute | solution.py:24
  115.0 0.0 copy-start.4
  115.1 7.5 %collective-permute-start.3 = (f32[1,2,8,2304]{3,2,1,0:T(8,128)S(1)}, f32[1,2,8,2304]{3,2,1,0:T(8,128)S(1)}, u32[]{:S(2)}, u32[]{:S(2)}) collective-permute-start(f32[1,2,8,2304]{3,2,1,0:T(8,128)S(1)} %get-tuple-element.31), channel_id=1, source_target_pairs={{0,1},{1,2},{2,3},{4,5},{5,6},{6,7},{8,9},{9,10},{10,11},{12,13},{... | collective-permute-start | bytes 442376 | tf_op jit(solution)/shard_map/ppermute | solution.py:21
  122.6 0.6 fusion.58
  123.3 0.1 collective-permute-done.2
  123.4 1.7 %collective-permute-done.3 = f32[1,2,8,2304]{3,2,1,0:T(8,128)S(1)} collective-permute-done((f32[1,2,8,2304]{3,2,1,0:T(8,128)S(1)}, f32[1,2,8,2304]{3,2,1,0:T(8,128)S(1)}, u32[]{:S(2)}, u32[]{:S(2)}) %collective-permute-start.3) | collective-permute-done | bytes 147488 | tf_op jit(solution)/shard_map/ppermute | solution.py:21
  125.1 0.0 copy-done.4
  125.1 2.1 %fusion.22 = f32[12,2,8,2304]{3,2,1,0:T(8,128)S(1)} fusion(f32[12,2,8,2304]{3,2,1,0:T(8,128)S(1)} %multiply_add_fusion.1, f32[1,2,8,2304]{3,2,1,0:T(8,128)S(1)} %collective-permute-done.3, f32[1,2,8,2304]{3,2,1,0:T(8,128)S(1)} %collective-permute-done.2, f32[12,2,8,2303]{3,2,1,0:T(8,128)S(1)} %get-tuple-element.29, ...), kind=kLoop, calls=%fused_computation.44 | loop fusion | flops 10616832 | bytes 11576384 | tf_op jit(solution)/shard_map/div | solution.py:159
  127.2 0.6 fusion.56
  127.8 1.9 %collective-permute-start.4 = (f32[1,2,8,2304]{3,2,1,0:T(8,128)S(1)}, f32[1,2,8,2304]{3,2,1,0:T(8,128)S(1)}, u32[]{:S(2)}, u32[]{:S(2)}) collective-permute-start(f32[1,2,8,2304]{3,2,1,0:T(8,128)S(1)} %get-tuple-element.24), channel_id=1, source_target_pairs={{1,0},{2,1},{3,2},{5,4},{6,5},{7,6},{9,8},{10,9},{11,10},{13,12},{... | collective-permute-start | bytes 442376 | tf_op jit(solution)/shard_map/ppermute | solution.py:24
  129.8 8.4 %collective-permute-start.5 = (f32[1,2,8,2304]{3,2,1,0:T(8,128)S(1)}, f32[1,2,8,2304]{3,2,1,0:T(8,128)S(1)}, u32[]{:S(2)}, u32[]{:S(2)}) collective-permute-start(f32[1,2,8,2304]{3,2,1,0:T(8,128)S(1)} %get-tuple-element.25), channel_id=1, source_target_pairs={{0,1},{1,2},{2,3},{4,5},{5,6},{6,7},{8,9},{9,10},{10,11},{12,13},{... | collective-permute-start | bytes 442376 | tf_op jit(solution)/shard_map/ppermute | solution.py:21
  138.2 0.6 fusion.55
  138.8 0.4 collective-permute-done.4
  139.2 2.3 %collective-permute-done.5 = f32[1,2,8,2304]{3,2,1,0:T(8,128)S(1)} collective-permute-done((f32[1,2,8,2304]{3,2,1,0:T(8,128)S(1)}, f32[1,2,8,2304]{3,2,1,0:T(8,128)S(1)}, u32[]{:S(2)}, u32[]{:S(2)}) %collective-permute-start.5) | collective-permute-done | bytes 147488 | tf_op jit(solution)/shard_map/ppermute | solution.py:21
  141.5 2.0 %fusion.16 = f32[12,2,8,2304]{3,2,1,0:T(8,128)S(1)} fusion(f32[12,2,8,2304]{3,2,1,0:T(8,128)S(1)} %fusion.22, f32[1,2,8,2304]{3,2,1,0:T(8,128)S(1)} %collective-permute-done.5, f32[1,2,8,2304]{3,2,1,0:T(8,128)S(1)} %collective-permute-done.4, f32[12,2,8,2303]{3,2,1,0:T(8,128)S(1)} %get-tuple-element.23, f32[12,2,8,2303]{3,2,1,0:T(8,128)S(1)} %get-tuple-element.22, ...), kind=kLoop, calls=%fused_computation.36 | loop fusion | flops 10616832 | bytes 13345856 | tf_op jit(solution)/shard_map/div | solution.py:159
  143.6 0.6 fusion.53
  144.2 1.9 %collective-permute-start.6 = (f32[1,2,8,2304]{3,2,1,0:T(8,128)S(1)}, f32[1,2,8,2304]{3,2,1,0:T(8,128)S(1)}, u32[]{:S(2)}, u32[]{:S(2)}) collective-permute-start(f32[1,2,8,2304]{3,2,1,0:T(8,128)S(1)} %get-tuple-element.18), channel_id=1, source_target_pairs={{1,0},{2,1},{3,2},{5,4},{6,5},{7,6},{9,8},{10,9},{11,10},{13,12},{... | collective-permute-start | bytes 442376 | tf_op jit(solution)/shard_map/ppermute | solution.py:24
  146.1 8.4 %collective-permute-start.7 = (f32[1,2,8,2304]{3,2,1,0:T(8,128)S(1)}, f32[1,2,8,2304]{3,2,1,0:T(8,128)S(1)}, u32[]{:S(2)}, u32[]{:S(2)}) collective-permute-start(f32[1,2,8,2304]{3,2,1,0:T(8,128)S(1)} %get-tuple-element.19), channel_id=1, source_target_pairs={{0,1},{1,2},{2,3},{4,5},{5,6},{6,7},{8,9},{9,10},{10,11},{12,13},{... | collective-permute-start | bytes 442376 | tf_op jit(solution)/shard_map/ppermute | solution.py:21
  154.5 0.6 fusion.52
  155.1 0.4 collective-permute-done.6
  155.5 2.3 %collective-permute-done.7 = f32[1,2,8,2304]{3,2,1,0:T(8,128)S(1)} collective-permute-done((f32[1,2,8,2304]{3,2,1,0:T(8,128)S(1)}, f32[1,2,8,2304]{3,2,1,0:T(8,128)S(1)}, u32[]{:S(2)}, u32[]{:S(2)}) %collective-permute-start.7) | collective-permute-done | bytes 147488 | tf_op jit(solution)/shard_map/ppermute | solution.py:21
  157.8 2.9 %fusion.10 = f32[12,2,8,2304]{3,2,1,0:T(8,128)} fusion(f32[12,2,8,2304]{3,2,1,0:T(8,128)S(1)} %fusion.16, f32[1,2,8,2304]{3,2,1,0:T(8,128)S(1)} %collective-permute-done.7, f32[1,2,8,2304]{3,2,1,0:T(8,128)S(1)} %collective-permute-done.6, f32[12,2,8,2303]{3,2,1,0:T(8,128)S(1)} %get-tuple-element.17, f32[12,2,8,2303]{3,2,1,0:T(8,128)S(1)} %get-tuple-element.16, ...), kind=kLoop, calls=%fused_computation.28 | loop fusion | flops 10616832 | bytes 13345856 | tf_op jit(solution)/shard_map/div | solution.py:159
  (28 shorter events, 0.2 us)
Async XLA Ops:
  0.0 107.0 %collective-permute-start = (f32[12,2,8,2304]{3,2,1,0:T(8,128)}, f32[12,2,8,2304]{3,2,1,0:T(8,128)S(1)}, u32[]{:S(2)}, u32[]{:S(2)}) collective-permute-start(f32[12,2,8,2304]{3,2,1,0:T(8,128)} %param.2), channel_id=1, source_target_pairs={{4,0},{8,4},{12,8},{16,12},{20,16},{24,20},{28,24},{32,28},{36,32}... | collective-permute-start | bytes 5308424 | tf_op jit(solution)/shard_map/ppermute | solution.py:24
  13.5 93.5 %collective-permute-start.1 = (f32[12,2,8,2304]{3,2,1,0:T(8,128)}, f32[12,2,8,2304]{3,2,1,0:T(8,128)}, u32[]{:S(2)}, u32[]{:S(2)}) collective-permute-start(f32[12,2,8,2304]{3,2,1,0:T(8,128)} %param.2), channel_id=1, source_target_pairs={{0,4},{4,8},{8,12},{12,16},{16,20},{20,24},{24,28},{28,32},{32,36}... | collective-permute-start | bytes 5308424 | tf_op jit(solution)/shard_map/ppermute | solution.py:21
  16.6 0.6 copy-start.1
  16.8 0.6 copy-start.2
  16.9 0.6 copy-start.6
  17.5 89.5 %copy-start = (f32[12,2,8,2304]{3,2,1,0:T(8,128)S(1)}, f32[12,2,8,2304]{3,2,1,0:T(8,128)}, u32[]{:S(2)}) copy-start(f32[12,2,8,2304]{3,2,1,0:T(8,128)} %param.2) | copy-start | bytes 5308420
  97.0 0.6 copy-start.11
  112.9 10.5 %collective-permute-start.2 = (f32[1,2,8,2304]{3,2,1,0:T(8,128)S(1)}, f32[1,2,8,2304]{3,2,1,0:T(8,128)S(1)}, u32[]{:S(2)}, u32[]{:S(2)}) collective-permute-start(f32[1,2,8,2304]{3,2,1,0:T(8,128)S(1)} %get-tuple-element.30), channel_id=1, source_target_pairs={{1,0},{2,1},{3,2},{5,4},{6,5},{7,6},{9,8},{10,9},{11,10},{13,12},{... | collective-permute-start | bytes 442376 | tf_op jit(solution)/shard_map/ppermute | solution.py:24
  115.0 10.0 %copy-start.3 = (f32[12,2,8]{2,1,0:T(2,128)S(1)}, f32[12,2,8]{2,1,0:T(2,128)}, u32[]{:S(2)}) copy-start(f32[12,2,8]{2,1,0:T(2,128)} %copy.11) | copy-start | bytes 2308
  115.0 10.0 %copy-start.4 = (f32[12,2,8]{2,1,0:T(2,128)S(1)}, f32[12,2,8]{2,1,0:T(2,128)}, u32[]{:S(2)}) copy-start(f32[12,2,8]{2,1,0:T(2,128)} %copy.12) | copy-start | bytes 2308
  115.1 10.0 %copy-start.5 = (f32[12,2,8]{2,1,0:T(2,128)S(1)}, f32[12,2,8]{2,1,0:T(2,128)}, u32[]{:S(2)}) copy-start(f32[12,2,8]{2,1,0:T(2,128)} %copy.10) | copy-start | bytes 2308
  115.1 10.0 %copy-start.7 = (f32[2,8]{1,0:T(2,128)S(1)}, f32[2,8]{1,0:T(2,128)}, u32[]{:S(2)}) copy-start(f32[2,8]{1,0:T(2,128)} %get-tuple-element.61) | copy-start | bytes 196
  115.1 10.0 %copy-start.8 = (f32[2,8]{1,0:T(2,128)S(1)}, f32[2,8]{1,0:T(2,128)}, u32[]{:S(2)}) copy-start(f32[2,8]{1,0:T(2,128)} %get-tuple-element.62) | copy-start | bytes 196
  115.1 10.0 %copy-start.9 = (f32[2,8]{1,0:T(2,128)S(1)}, f32[2,8]{1,0:T(2,128)}, u32[]{:S(2)}) copy-start(f32[2,8]{1,0:T(2,128)} %get-tuple-element.63) | copy-start | bytes 196
  115.1 10.0 %copy-start.10 = (f32[2,8]{1,0:T(2,128)S(1)}, f32[2,8]{1,0:T(2,128)}, u32[]{:S(2)}) copy-start(f32[2,8]{1,0:T(2,128)} %get-tuple-element.65) | copy-start | bytes 196
  115.1 10.0 %collective-permute-start.3 = (f32[1,2,8,2304]{3,2,1,0:T(8,128)S(1)}, f32[1,2,8,2304]{3,2,1,0:T(8,128)S(1)}, u32[]{:S(2)}, u32[]{:S(2)}) collective-permute-start(f32[1,2,8,2304]{3,2,1,0:T(8,128)S(1)} %get-tuple-element.31), channel_id=1, source_target_pairs={{0,1},{1,2},{2,3},{4,5},{5,6},{6,7},{8,9},{9,10},{10,11},{12,13},{... | collective-permute-start | bytes 442376 | tf_op jit(solution)/shard_map/ppermute | solution.py:21
  127.8 11.3 %collective-permute-start.4 = (f32[1,2,8,2304]{3,2,1,0:T(8,128)S(1)}, f32[1,2,8,2304]{3,2,1,0:T(8,128)S(1)}, u32[]{:S(2)}, u32[]{:S(2)}) collective-permute-start(f32[1,2,8,2304]{3,2,1,0:T(8,128)S(1)} %get-tuple-element.24), channel_id=1, source_target_pairs={{1,0},{2,1},{3,2},{5,4},{6,5},{7,6},{9,8},{10,9},{11,10},{13,12},{... | collective-permute-start | bytes 442376 | tf_op jit(solution)/shard_map/ppermute | solution.py:24
  129.8 11.7 %collective-permute-start.5 = (f32[1,2,8,2304]{3,2,1,0:T(8,128)S(1)}, f32[1,2,8,2304]{3,2,1,0:T(8,128)S(1)}, u32[]{:S(2)}, u32[]{:S(2)}) collective-permute-start(f32[1,2,8,2304]{3,2,1,0:T(8,128)S(1)} %get-tuple-element.25), channel_id=1, source_target_pairs={{0,1},{1,2},{2,3},{4,5},{5,6},{6,7},{8,9},{9,10},{10,11},{12,13},{... | collective-permute-start | bytes 442376 | tf_op jit(solution)/shard_map/ppermute | solution.py:21
  144.2 11.3 %collective-permute-start.6 = (f32[1,2,8,2304]{3,2,1,0:T(8,128)S(1)}, f32[1,2,8,2304]{3,2,1,0:T(8,128)S(1)}, u32[]{:S(2)}, u32[]{:S(2)}) collective-permute-start(f32[1,2,8,2304]{3,2,1,0:T(8,128)S(1)} %get-tuple-element.18), channel_id=1, source_target_pairs={{1,0},{2,1},{3,2},{5,4},{6,5},{7,6},{9,8},{10,9},{11,10},{13,12},{... | collective-permute-start | bytes 442376 | tf_op jit(solution)/shard_map/ppermute | solution.py:24
  146.1 11.7 %collective-permute-start.7 = (f32[1,2,8,2304]{3,2,1,0:T(8,128)S(1)}, f32[1,2,8,2304]{3,2,1,0:T(8,128)S(1)}, u32[]{:S(2)}, u32[]{:S(2)}) collective-permute-start(f32[1,2,8,2304]{3,2,1,0:T(8,128)S(1)} %get-tuple-element.19), channel_id=1, source_target_pairs={{0,1},{1,2},{2,3},{4,5},{5,6},{6,7},{8,9},{9,10},{10,11},{12,13},{... | collective-permute-start | bytes 442376 | tf_op jit(solution)/shard_map/ppermute | solution.py:21
